TPU v7x, 128 devices: a whole 4x4x4 slice. The times are simulated.
128 devices in a mesh: group: 8 (over y, core), shard: 16 (over x, z).
Axes of the slice: x: 4, y: 4, z: 4, core: 2. Of those that a mesh axis runs over, the one named last changes fastest.
Arguments:
- tokens: bfloat16 [1024, 6144], P('group'), may hold values from -6 to 6
- experts: int32 [1024, 2], P('group'), may hold values from 0 to 7, all different within a row; in each aligned block of 128 rows (0 to 127, 128 to 255, ...) at most 64 rows name the same one
- mix_weight: float32 [1024, 2], P('group'), may hold values from 0.2 to 1
- w_gate: bfloat16 [8, 6144, 8192], P('group', None, 'shard'), may hold values from -0.078125 to 0.078125
- w_up: bfloat16 [8, 6144, 8192], P('group', None, 'shard'), may hold values from -0.078125 to 0.078125
- w_down: bfloat16 [8, 8192, 6144], P('group', 'shard'), may hold values from -0.09375 to 0.09375
Outputs:
- mixed: bfloat16 [1024, 6144], P('group', 'shard')
Inputs may be any that keep to these rules, and one draw needn't show every extreme that they name: Each token names 2 different experts. Among the tokens of one group no expert is named more than 64 times, a bound that some block reaches.
All inputs are finite; a program needn't handle non-finite values.
Results may differ from a plain program's by a relative error of at most 0.02.
Values may be sent and summed in bfloat16 or wider, within the bound.
A program may use at most 128 MiB of HBM per device.

v0:
```python
import jax
import jax.numpy as jnp
from jax import lax
from jax.sharding import PartitionSpec as P


def slot_plan(chosen, experts_total, capacity, reach):
    count = chosen.shape[0]
    labels = jnp.arange(experts_total, dtype=jnp.int32)
    onehot = (chosen[:, None] == labels[None, :]).astype(jnp.int32)
    before = jnp.cumsum(onehot, axis=0) - onehot
    slot_rank = jnp.sum(before * onehot, axis=1)
    route_ids = jnp.arange(count, dtype=jnp.int32)
    slots = jnp.arange(capacity, dtype=jnp.int32)
    matches = (chosen[None, None, :] == labels[:, None, None]) & (
        slot_rank[None, None, :] == slots[None, :, None]
    )
    filled = jnp.any(matches, axis=2)
    source_row = jnp.sum(jnp.where(matches, route_ids[None, None, :] // reach, 0), axis=2)
    return (slot_rank, source_row, filled)


def local(tokens, experts, mix_weight, w_gate, w_up, w_down):
    groups = lax.axis_size("group")
    count, width = tokens.shape
    reach = experts.shape[1]
    capacity = count // 2
    chosen = experts.reshape(-1)
    slot_rank, source_row, filled = slot_plan(chosen, groups, capacity, reach)
    outgoing = jnp.where(filled[:, :, None], tokens[source_row], jnp.zeros((), tokens.dtype))
    arrived = lax.all_to_all(outgoing, "group", split_axis=0, concat_axis=0, tiled=True)
    flat_rows = arrived.reshape(-1, width)
    gate = jnp.dot(flat_rows, w_gate[0], preferred_element_type=jnp.float32)
    up = jnp.dot(flat_rows, w_up[0], preferred_element_type=jnp.float32)
    hidden = (jax.nn.silu(gate) * up).astype(jnp.bfloat16)
    partial_value = jnp.dot(hidden, w_down[0], preferred_element_type=jnp.float32).astype(
        jnp.bfloat16
    )
    partial_value = partial_value.reshape(arrived.shape)
    summed = (
        lax.psum_scatter(partial_value, "shard", scatter_dimension=2, tiled=True)
        .astype(jnp.float32)
        .astype(jnp.bfloat16)
    )
    returned = lax.all_to_all(summed, "group", split_axis=0, concat_axis=0, tiled=True)
    picked = returned[chosen, slot_rank].reshape(count, reach, -1).astype(jnp.float32)
    mixed = jnp.sum(mix_weight[:, :, None] * picked, axis=1)
    return mixed.astype(jnp.bfloat16)


def solution(mesh):
    placed = (
        P("group", None),
        P("group", None),
        P("group", None),
        P("group", None, "shard"),
        P("group", None, "shard"),
        P("group", "shard", None),
    )
    return jax.shard_map(
        local, mesh=mesh, in_specs=placed, out_specs=P("group", "shard"), check_vma=False
    )
```

profile of v0, /device:TPU:0, one launch (start us, length us, event | category | flops | bytes accessed | tf_op | source)
XLA Modules:
  0.0 248.5 jit_solution(12717497433101713569)
XLA Ops:
  6.5 0.0 copy-start
  6.5 0.0 reduce-scatter.4.cloned.1.call-start
  6.5 0.9 copy.17
  7.4 0.1 eq.61
  7.6 0.1 eq.68
  7.8 0.6 reduce-window.6
  8.3 0.2 slice_reduce_fusion
  8.6 0.1 fusion.13
  8.7 0.2 and_reduce_fusion
  8.9 0.2 fusion.11
  9.2 0.1 reshape.178
  9.3 0.0 copy-done
  9.3 6.1 %gather_fusion = bf16[512,6144]{1,0:T(8,128)(2,1)} fusion(bf16[128,6144]{1,0:T(8,128)(2,1)S(1)} %copy-done, s32[1024]{0:T(1024)S(1)} %pad_clamp_fusion), kind=kCustom, calls=%fused_computation | custom fusion | bytes 12584960 | tf_op jit(solution)/shard_map/gather | solution.py:30
  15.4 0.0 slice-start
  15.4 3.4 %broadcast_select_fusion = bf16[8,64,6144]{2,1,0:T(8,128)(2,1)S(1)} fusion(bf16[8,64,6144]{2,1,0:T(8,128)(2,1)} %bitcast.36, pred[8,64]{1,0:T(8,128)(4,1)S(1)} %and_reduce_fusion), kind=kLoop, calls=%fused_computation.8 | loop fusion | flops 3145728 | bytes 12583424 | tf_op jit(solution)/shard_map/jit(_where)/select_n | solution.py:30
  18.8 0.0 slice-start.1
  18.8 0.0 slice-start.2
  18.8 77.8 %all_to_all.10 = bf16[8,64,6144]{2,1,0:T(8,128)(2,1)S(1)} all-to-all(bf16[8,64,6144]{2,1,0:T(8,128)(2,1)S(1)} %broadcast_select_fusion), channel_id=1, replica_groups=mesh['group'=8,'shard'=16] {'group'}, dimensions={0} | all-to-all | bytes 12582912 | tf_op jit(solution)/shard_map/all_to_all | solution.py:31
  96.6 0.0 slice-done
  96.6 0.0 slice-done.1
  96.6 0.0 slice-start.3
  96.6 0.0 slice-start.4
  96.6 3.4 %fusion.3 = f32[512,512]{1,0:T(8,128)S(1)} fusion(bf16[512,6144]{1,0:T(8,128)(2,1)S(1)} %bitcast.38, bf16[1,6144,512]{2,1,0:T(8,128)(2,1)S(1)} %bitcast.44), kind=kOutput, calls=%fused_computation.6 | convolution fusion | flops 3221225472 | bytes 13631488 | tf_op jit(solution)/shard_map/dot_general | solution.py:33
  100.0 0.0 slice-done.2
  100.0 0.0 slice-done.3
  100.0 0.0 slice-start.5
  100.0 3.5 %fusion.8 = bf16[512,512]{1,0:T(8,128)(2,1)S(1)} fusion(bf16[512,6144]{1,0:T(8,128)(2,1)S(1)} %bitcast.39, bf16[1,6144,512]{2,1,0:T(8,128)(2,1)S(1)} %bitcast.46, f32[512,512]{1,0:T(8,128)S(1)} %fusion.3), kind=kOutput, calls=%fused_computation.10 | convolution fusion | flops 3222798336 | bytes 14155776 | tf_op jit(solution)/shard_map/dot_general | solution.py:34
  103.5 0.0 slice-done.4
  103.5 0.0 slice-done.5
  103.6 5.4 %convolution_convert_fusion = bf16[512,6144]{1,0:T(8,128)(2,1)} fusion(bf16[512,512]{1,0:T(8,128)(2,1)S(1)} %fusion.8, bf16[1,512,6144]{2,1,0:T(8,128)(2,1)S(1)} %bitcast.48), kind=kOutput, calls=%fused_computation.2 | convolution fusion | flops 3224371200 | bytes 13107200 | tf_op jit(solution)/shard_map/dot_general | solution.py:36
  108.9 14.3 %copy.20 = bf16[8,64,6144]{1,0,2:T(8,128)(2,1)} copy(bf16[8,64,6144]{2,1,0:T(8,128)(2,1)} %bitcast.40) | data formatting | bytes 12582912
  123.3 17.1 %reshape.191 = bf16[6144,512]{1,0:T(8,128)(2,1)} reshape(bf16[6144,8,64]{2,1,0:T(8,128)(2,1)} %bitcast.35) | data formatting | bytes 12582912
  140.4 0.0 copy-start.2
  140.4 0.0 copy-start.1
  140.4 0.0 reduce-scatter.4.cloned.1.call-update
  140.4 82.0 %reduce-scatter.4.cloned.1.call-done = bf16[384,512]{1,0:T(8,128)(2,1)} async-done(((bf16[6144,512]{1,0:T(8,128)(2,1)}), bf16[384,512]{1,0:T(8,128)(2,1)}) %reduce-scatter.4.cloned.1.call-update) | async-done | bytes 393232
  222.4 1.5 reshape.192
  223.9 1.2 copy.21
  225.2 4.3 %all-to-all-start.1 = ((bf16[8,64,384]{2,1,0:T(8,128)(2,1)}), bf16[8,64,384]{2,1,0:T(8,128)(2,1)S(1)}, u32[]{:S(2)}, u32[]{:S(2)}) async-start(bf16[8,64,384]{2,1,0:T(8,128)(2,1)} %copy.21), calls=%async_computation.1 | async-start | bytes 786432 | tf_op jit(solution)/shard_map/all_to_all | solution.py:45
  229.4 0.1 reshape.174
  229.6 0.0 copy-done.2
  229.6 0.1 copy.16
  229.7 8.7 %all-to-all-done.1 = bf16[8,64,384]{2,1,0:T(8,128)(2,1)S(1)} async-done(((bf16[8,64,384]{2,1,0:T(8,128)(2,1)}), bf16[8,64,384]{2,1,0:T(8,128)(2,1)S(1)}, u32[]{:S(2)}, u32[]{:S(2)}) %all-to-all-start.1) | async-done | bytes 393248 | tf_op jit(solution)/shard_map/all_to_all | solution.py:45
  238.4 1.9 gather_fusion.1
  240.3 0.2 reshape.175
  240.5 1.2 multiply_reduce_fusion
  241.6 0.0 copy-done.1
  (12 shorter events, 0.1 us)
Async XLA Ops:
  6.5 2.7 %copy-start = (bf16[128,6144]{1,0:T(8,128)(2,1)S(1)}, bf16[128,6144]{1,0:T(8,128)(2,1)}, u32[]{:S(2)}) copy-start(bf16[128,6144]{1,0:T(8,128)(2,1)} %param.6) | copy-start | bytes 4718596
  6.5 215.9 %reduce-scatter.4.cloned.1.call-start = ((), (), s32[]{:S(2)}) async-start(), calls=%async_computation.3 | async-start | bytes 6684672
  15.4 81.2 %slice-start = ((s8[6291456]{0:T(1024)(128)(4,1)}), s8[4194304]{0:T(1024)(128)(4,1)S(1)}, s32[]{:S(2)}) async-start(s8[6291456]{0:T(1024)(128)(4,1)} %bitcast.43), calls=%async_computation.4 | async-start | bytes 8388608
  18.8 77.8 %slice-start.1 = ((s8[6291456]{0:T(1024)(128)(4,1)}), s8[2097152]{0:T(1024)(128)(4,1)S(1)}, s32[]{:S(2)}) async-start(s8[6291456]{0:T(1024)(128)(4,1)} %bitcast.43), calls=%async_computation.5 | async-start | bytes 4194304
  18.8 81.2 %slice-start.2 = ((s8[6291456]{0:T(1024)(128)(4,1)}), s8[4194304]{0:T(1024)(128)(4,1)S(1)}, s32[]{:S(2)}) async-start(s8[6291456]{0:T(1024)(128)(4,1)} %bitcast.45), calls=%async_computation.6 | async-start | bytes 8388608
  96.6 3.4 %slice-start.3 = ((s8[6291456]{0:T(1024)(128)(4,1)}), s8[2097152]{0:T(1024)(128)(4,1)S(1)}, s32[]{:S(2)}) async-start(s8[6291456]{0:T(1024)(128)(4,1)} %bitcast.45), calls=%async_computation.7 | async-start | bytes 4194304
  96.6 6.9 %slice-start.4 = ((s8[6291456]{0:T(1024)(128)(4,1)}), s8[4194304]{0:T(1024)(128)(4,1)S(1)}, s32[]{:S(2)}) async-start(s8[6291456]{0:T(1024)(128)(4,1)} %bitcast.47), calls=%async_computation.8 | async-start | bytes 8388608
  100.0 3.5 %slice-start.5 = ((s8[6291456]{0:T(1024)(128)(4,1)}), s8[2097152]{0:T(1024)(128)(4,1)S(1)}, s32[]{:S(2)}) async-start(s8[6291456]{0:T(1024)(128)(4,1)} %bitcast.47), calls=%async_computation.9 | async-start | bytes 4194304
  140.4 89.2 %copy-start.2 = (f32[128,2]{0,1:T(2,128)S(1)}, f32[128,2]{0,1:T(2,128)}, u32[]{:S(2)}) copy-start(f32[128,2]{0,1:T(2,128)} %param.8) | copy-start | bytes 3076
  140.4 101.2 %copy-start.1 = (bf16[128,6144]{1,0:T(8,128)(2,1)S(1)}, bf16[128,6144]{1,0:T(8,128)(2,1)}, u32[]{:S(2)}) copy-start(bf16[128,6144]{1,0:T(8,128)(2,1)} %param.6) | copy-start | bytes 4718596
  225.2 13.2 %all-to-all-start.1 = ((bf16[8,64,384]{2,1,0:T(8,128)(2,1)}), bf16[8,64,384]{2,1,0:T(8,128)(2,1)S(1)}, u32[]{:S(2)}, u32[]{:S(2)}) async-start(bf16[8,64,384]{2,1,0:T(8,128)(2,1)} %copy.21), calls=%async_computation.1 | async-start | bytes 786432 | tf_op jit(solution)/shard_map/all_to_all | solution.py:45
Sparse Core Ops, SparseCore 0:
  140.5 81.8 reduce-scatter.3
where the time goes:
time: 250 us; the launch traced here: 248 us
  waiting for transfers between devices  90.7 us (36%)
  blocking collectives  77.8 us (31%)
  local copies, waits for them, and re-layouts  44.2 us (18%)
  between operations  13.6 us (5%)
  matrix products  12.2 us (5%)
  other arithmetic  5.8 us (2%)
  starting transfers between devices  4.27 us (2%)
    unnamed x2, waiting for transfers between devices  82 us
    all_to_all x1, blocking collectives, local(): lax.all_to_all(outgoing, 'group', split_axis=0, concat_axis=0, tiled=True)  77.8 us
    unnamed x24, local copies, waits for them, and re-layouts  35.3 us
    all_to_all x1, waiting for transfers between devices, local(): lax.all_to_all(summed, 'group', split_axis=0, concat_axis=0, tiled=True)  8.67 us
    gather x1, local copies, waits for them, and re-layouts, local(): tokens[source_row]  6.09 us
    dot_general x1, matrix products, local(): jnp.dot(hidden, w_down[0], preferred_element_type=jnp.float32)  5.36 us
  transfers between devices with their start and end apart: 2, of which 2 were waited for; matrix products, arithmetic and copies ran while one was open for 0% of the time, Pallas kernels for 0%

commit v1 on v0

v1 whole, which is shorter than its diff:
```python
import functools

import jax
import jax.numpy as jnp
from jax import lax
from jax.experimental import pallas as pl
from jax.experimental.pallas import tpu as pltpu
from jax.sharding import PartitionSpec as P

MESH = pl.DeviceIdType.MESH
F32, BF16 = jnp.float32, jnp.bfloat16
NX = 4
TG = 128
CAP = 64
KB = 768
FFS = 512
HALF = 3072
CHUNKS = 2
ROWS = TG // CHUNKS
COLS = 512


def kernel(
    tok, ex, mw, wg_hbm, wu_hbm, wd_hbm, out,
    wg, wu, wd, land, meta, pick, back, wslot, xown, xsend, xsib, acc_g, acc_u, hid,
    pcat, psend, t0, t1, t2, rb1, rb2, rb3,
    local_sem, send_sem, recv_sem,
):
    group, shard = lax.axis_index("group"), lax.axis_index("shard")
    x, y, z, c = shard // NX, group // 2, shard % NX, group % 2
    sib = 1 - c

    def dev(x, y, z, c):
        return ((y % NX) * 2 + c, (x % NX) * NX + z % NX)

    def on_ring(d):
        return dev(x + d * (1 - c) + NX, y, z + d * c + NX, c)

    def ring_place(core):
        return x * (1 - core) + z * core

    r = ring_place(c)

    used = [0]

    def remote(src, dst, device):
        i = used[0]
        used[0] += 1
        return pltpu.make_async_remote_copy(
            src_ref=src, dst_ref=dst, send_sem=send_sem.at[i], recv_sem=recv_sem.at[i],
            device_id=device, device_id_type=MESH,
        )

    sent = []

    def go(copy):
        copy.start()
        sent.append(copy)
        return copy

    peers = [((y + dy) % NX, c if dc == 0 else sib) for dy in range(NX) for dc in range(2) if dy or dc]
    partners = [dev(x, py, z, pc) for py, pc in peers]
    partners += [dev(x + 1, y, z, c), dev(x + NX - 1, y, z, c), dev(x, y, z + 1, c), dev(x, y, z + NX - 1, c)]
    barrier = pltpu.get_barrier_semaphore()
    for partner in partners:
        pl.semaphore_signal(barrier, inc=1, device_id=partner, device_id_type=MESH)

    load_g = pltpu.make_async_copy(wg_hbm.at[0], wg, local_sem.at[0])
    load_u = pltpu.make_async_copy(wu_hbm.at[0], wu, local_sem.at[1])
    own_loads = [
        pltpu.make_async_copy(
            tok.at[:, pl.ds(pl.multiple_of(c * HALF + q * KB, KB), KB)], land.at[q, y, c], local_sem.at[3 + q]
        )
        for q in range(NX)
    ]
    for copy in own_loads:
        copy.start()

    meta[group] = jnp.zeros((8, TG), F32)
    meta[group, 0:2] = ex[...].astype(F32)
    meta[group, 2:4] = mw[...]

    pl.semaphore_wait(barrier, len(partners))

    plans = [go(remote(meta.at[group], meta.at[group], dev(x, py, z, pc))) for py, pc in peers]

    def token_block(core, q, h):
        return tok.at[pl.ds(h * ROWS, ROWS), pl.ds(pl.multiple_of(core * HALF + q * KB, KB), KB)]

    direct = {}
    for h in range(CHUNKS):
        for step in (1, -1):
            for dc in range(2):
                core = c if dc == 0 else sib
                q = ring_place(core)
                direct[h, step, dc] = go(
                    remote(
                        token_block(core, q, h),
                        land.at[q, y, c, pl.ds(h * ROWS, ROWS)],
                        dev(x, y + step + NX, z, core),
                    )
                )
    load_g.start()
    load_u.start()
    across = [
        go(
            remote(
                tok.at[:, pl.ds(pl.multiple_of(sib * HALF + q * KB, KB), KB)], land.at[q, y, c], dev(x, y, z, sib)
            )
        )
        for q in range(NX)
    ]

    def load_down(i, carry):
        j, b = i // 16, i % 16
        place = jnp.where(j == 2, (b % NX) * NX + b // NX, b)
        pltpu.make_async_copy(
            wd_hbm.at[0, :, pl.ds(pl.multiple_of(b * 384 + j * 128, 128), 128)],
            wd.at[j, :, pl.ds(pl.multiple_of(place * 128, 128), 128)],
            local_sem.at[2],
        ).start()
        return carry

    lax.fori_loop(0, 48, load_down, 0)

    for copy in plans:
        copy.wait_recv()
    own_e = group.astype(F32)
    sib_e = (2 * y + sib).astype(F32)
    before = lax.broadcasted_iota(jnp.int32, (TG, TG), 0) < lax.broadcasted_iota(jnp.int32, (TG, TG), 1)
    before = jnp.where(before, 1.0, 0.0).astype(BF16)
    slot = lax.broadcasted_iota(jnp.int32, (CAP, TG), 0).astype(F32)
    first, second = meta[:, 0, :], meta[:, 1, :]
    first_w, second_w = meta[:, 2, :], meta[:, 3, :]
    plan = []
    for e in (own_e, sib_e):
        named = jnp.where((first == e) | (second == e), 1.0, 0.0)
        rank = jnp.dot(named.astype(BF16), before, preferred_element_type=F32)
        plan.append(jnp.where(named > 0.5, rank, -1.0))
    weight = jnp.where(first == own_e, first_w, 0.0) + jnp.where(second == own_e, second_w, 0.0)
    for g in range(8):
        py, pc = g // 2, g % 2
        rows = [jnp.where(p[g : g + 1, :] == slot, 1.0, 0.0) for p in plan]
        onehot = jnp.concatenate(rows, axis=0)
        pick[g] = onehot.astype(BF16)
        back[pc, py] = onehot.T.astype(BF16)
        total = jnp.sum(rows[0] * weight[g : g + 1, :], axis=1, keepdims=True)
        wslot[pl.ds((pc * 4 + py) * CAP, CAP)] = jnp.broadcast_to(total, (CAP, 128))

    ring_own, relay_y, ring_relay = {}, {}, {}

    def forward(h, dy):
        block = land.at[r, (y + dy) % NX, :, pl.ds(h * ROWS, ROWS)]
        for d in (1, -1):
            ring_own[h, dy, d] = go(remote(block, block, on_ring(d)))

    for h in range(CHUNKS):
        for dy, step in ((3, 1), (1, -1)):
            for dc in range(2):
                direct[h, step, dc].wait_recv()
            block = land.at[r, (y + dy) % NX, 1 if step == 1 else 0, pl.ds(h * ROWS, ROWS)]
            relay_y[h, step] = go(remote(block, block, dev(x, y + step + NX, z, c)))
            forward(h, dy)

    def pass_on(h, dy):
        for d in (1, -1):
            ring_own[h, dy, d].wait_recv()
            block = land.at[(r - d + NX) % NX, (y + dy) % NX, 1 if d == 1 else 0, pl.ds(h * ROWS, ROWS)]
            ring_relay[h, dy, d] = go(remote(block, block, on_ring(d)))

    for h in range(CHUNKS):
        for step in (1, -1):
            relay_y[h, step].wait_recv()
        forward(h, 2)
        for dy in (3, 1):
            pass_on(h, dy)
    for copy in own_loads:
        copy.wait()
    for copy in across:
        copy.wait_recv()
    load_g.wait()
    load_u.wait()

    acc_g[...] = jnp.zeros_like(acc_g)
    acc_u[...] = jnp.zeros_like(acc_u)
    cross = []

    def select(i, q):
        def one(g, carry):
            py, pc = g // 2, g % 2
            rows = jnp.dot(pick[g], land[q, py, pc], preferred_element_type=F32).astype(BF16)
            place = pl.ds(pl.multiple_of((pc * 4 + py) * CAP, CAP), CAP)
            xown[place, :] = rows[0:CAP]
            xsend[i, place, :] = rows[CAP:]
            return carry

        lax.fori_loop(0, 8, one, 0)
        cross.append(go(remote(xsend.at[i], xsib.at[i], dev(x, y, z, sib))))

    def gate_up(rows_ref, start):
        depth = pl.ds(pl.multiple_of(start, KB), KB)

        def one(m, carry):
            place = pl.ds(pl.multiple_of(m * 256, 256), 256)
            rows = rows_ref[place, :]
            acc_g[place, :] += jnp.dot(rows, wg[depth, :], preferred_element_type=F32)
            acc_u[place, :] += jnp.dot(rows, wu[depth, :], preferred_element_type=F32)
            return carry

        lax.fori_loop(0, 2, one, 0)

    order = (0, 1, 3, 2)
    places = [(r + d) % NX for d in order]
    sib_places = [(ring_place(sib) + d) % NX for d in order]

    def own_block(i):
        select(i, places[i])
        gate_up(xown, c * HALF + places[i] * KB)

    def sib_block(i):
        cross[i].wait_recv()
        gate_up(xsib.at[i], sib * HALF + sib_places[i] * KB)

    own_block(0)
    for h in range(CHUNKS):
        pass_on(h, 2)
    own_block(1)
    own_block(2)
    sib_block(0)
    sib_block(1)
    for h in range(CHUNKS):
        for dy in (3, 1, 2):
            for d in (1, -1):
                ring_relay[h, dy, d].wait_recv()
    own_block(3)
    sib_block(2)
    sib_block(3)

    def activate(m, carry):
        place = pl.ds(pl.multiple_of(m * 128, 128), 128)
        gate, up = acc_g[place, :], acc_u[place, :]
        hid[place, :] = (jax.nn.silu(gate) * up * wslot[place, 0:1]).astype(BF16)
        return carry

    lax.fori_loop(0, 4, activate, 0)

    pltpu.make_async_copy(wd, wd, local_sem.at[2]).wait()
    ts = (t0, t1, t2)
    at = ((x, y, z), (y, z, x), (z, x, y))
    steps = (
        (lambda d: dev(x + d + NX, y, z, c)),
        (lambda d: dev(x, y + d + NX, z, c)),
        (lambda d: dev(x, y, z + d + NX, c)),
    )
    swap = {}

    def down(n, j, a):
        columns = pl.ds(pl.multiple_of(a * COLS, COLS), COLS)
        w = wd[j, :, columns]
        theirs = jnp.dot(hid[pl.ds(pl.multiple_of(sib * 256, 256), 256), :], w, preferred_element_type=F32)
        psend[n] = theirs.astype(BF16).reshape(4, CAP, COLS)
        swap[n] = go(remote(psend.at[n], pcat.at[n, :, pl.ds(CAP, CAP), :], dev(x, y, z, sib)))
        ours = jnp.dot(hid[pl.ds(pl.multiple_of(c * 256, 256), 256), :], w, preferred_element_type=F32)
        pcat[n, :, 0:CAP, :] = ours.astype(BF16).reshape(4, CAP, COLS)

    def combine(n, j, a):
        swap[n].wait_recv()
        for py in range(4):
            rows = jnp.dot(back[c, py], pcat[n, py], preferred_element_type=F32).astype(BF16)
            for b in range(4):
                part = rows[:, b * 128 : (b + 1) * 128]
                if j == 0:
                    t0[a, py, b] = part
                elif j == 1:
                    t1[py, b, a] = part
                else:
                    t2[a, b, py] = part

    copies = {}

    def start(j, level, t, buf, place, axis, kind):
        size = t.shape[1] // 2
        far, right, left = (place + 2) % NX, (place + 1) % NX, (place + 3) % NX
        low, high = pl.ds(0, size), pl.ds(size, size)
        src = {
            "R1a": t.at[far, low], "L1a": t.at[far, high], "R1b": t.at[right, high],
            "L1b": t.at[left, low], "R2": t.at[right, low], "L2": t.at[left, high],
        }[kind]
        slot_of = ("R1a", "L1a", "R1b", "L1b", "R2", "L2").index(kind)
        copies[j, level, kind] = go(remote(src, buf.at[j, slot_of], steps[axis](1 if kind[0] == "R" else -1)))

    def add(t, index, low, size, *bufs):
        place = pl.ds(low, size)
        total = t[index, place].astype(F32)
        for buf in bufs:
            total = total + buf[...].astype(F32)
        t[index, place] = total.astype(BF16)

    def middle(j, level, t, buf, place, axis):
        size = t.shape[1] // 2
        copies[j, level, "R1a"].wait_recv()
        add(t, (place + 1) % NX, 0, size, buf.at[j, 0])
        start(j, level, t, buf, place, axis, "R2")
        copies[j, level, "L1a"].wait_recv()
        add(t, (place + 3) % NX, size, size, buf.at[j, 1])
        start(j, level, t, buf, place, axis, "L2")

    def finish(j, level, t, buf, place, axis):
        size = t.shape[1] // 2
        for kind in ("R1b", "L1b", "R2", "L2"):
            copies[j, level, kind].wait_recv()
        add(t, place, 0, size, buf.at[j, 4], buf.at[j, 3])
        add(t, place, size, size, buf.at[j, 2], buf.at[j, 5])

    axes = ((0, 1, 2), (1, 2, 0), (2, 0, 1))

    def args(j, level):
        t = ts[j]
        for l in range(level):
            t = t.at[at[j][l]]
        return (j, level, t, (rb1, rb2, rb3)[level], at[j][level], axes[j][level])

    chunks = [(1, 0, 0), (1, 0, 1), (1, 0, 2), (1, 0, 3)]
    chunks += [(0, x, 2), (2, z, 2), (0, x, 1), (0, x, 3), (2, z, 1), (2, z, 3), (0, x, 0), (2, z, 0)]

    def after(j, k):
        if j == 1:
            if k == 3:
                for kind in ("R1a", "L1a", "R1b", "L1b"):
                    start(*args(1, 0), kind)
        elif k == 2:
            start(*args(j, 0), "R1a")
            start(*args(j, 0), "L1a")
        elif k == 1:
            start(*args(j, 0), "R1b")
        elif k == 3:
            start(*args(j, 0), "L1b")

    lag = 1
    for n in range(len(chunks) + lag):
        if n < len(chunks):
            j, base, k = chunks[n]
            down(n, j, (base + k) % NX)
        if n >= lag:
            j, base, k = chunks[n - lag]
            combine(n - lag, j, (base + k) % NX)
            after(j, k)

    for level in range(3):
        if level:
            for j in (1, 0, 2):
                for kind in ("R1a", "L1a", "R1b", "L1b"):
                    start(*args(j, level), kind)
        for j in (1, 0, 2):
            middle(*args(j, level))
        for j in (1, 0, 2):
            finish(*args(j, level))
    for j in range(3):
        out[:, j * 128 : (j + 1) * 128] = ts[j][at[j][0], at[j][1], at[j][2]]
    for copy in sent:
        copy.wait_send()


MESSAGES = 7 + 4 * CHUNKS + 4 + 2 * CHUNKS + 6 * CHUNKS + 6 * CHUNKS + 4 + 12 + 54


def local(tokens, experts, mix_weight, w_gate, w_up, w_down):
    any_spec = pl.BlockSpec(memory_space=pl.ANY)
    vmem_spec = pl.BlockSpec(memory_space=pltpu.VMEM)
    return pl.pallas_call(
        kernel,
        out_shape=jax.ShapeDtypeStruct((TG, 384), BF16),
        in_specs=[any_spec, vmem_spec, vmem_spec, any_spec, any_spec, any_spec],
        out_specs=vmem_spec,
        scratch_shapes=[
            pltpu.VMEM((6144, FFS), BF16),
            pltpu.VMEM((6144, FFS), BF16),
            pltpu.VMEM((3, FFS, 2048), BF16),
            pltpu.VMEM((4, 4, 2, TG, KB), BF16),
            pltpu.VMEM((8, 8, TG), F32),
            pltpu.VMEM((8, TG, TG), BF16),
            pltpu.VMEM((2, 4, TG, TG), BF16),
            pltpu.VMEM((512, 128), F32),
            pltpu.VMEM((512, KB), BF16),
            pltpu.VMEM((4, 512, KB), BF16),
            pltpu.VMEM((4, 512, KB), BF16),
            pltpu.VMEM((512, FFS), F32),
            pltpu.VMEM((512, FFS), F32),
            pltpu.VMEM((512, FFS), BF16),
            pltpu.VMEM((12, 4, 2 * CAP, COLS), BF16),
            pltpu.VMEM((12, 4, CAP, COLS), BF16),
            pltpu.VMEM((4, 4, 4, 128, 128), BF16),
            pltpu.VMEM((4, 4, 4, 128, 128), BF16),
            pltpu.VMEM((4, 4, 4, 128, 128), BF16),
            pltpu.VMEM((3, 6, 2, 4, 128, 128), BF16),
            pltpu.VMEM((3, 6, 2, 128, 128), BF16),
            pltpu.VMEM((3, 6, 64, 128), BF16),
            pltpu.SemaphoreType.DMA((7,)),
            pltpu.SemaphoreType.DMA((MESSAGES,)),
            pltpu.SemaphoreType.DMA((MESSAGES,)),
        ],
        compiler_params=pltpu.CompilerParams(
            collective_id=0, has_side_effects=True, vmem_limit_bytes=62 * 2**20
        ),
        name="expert_layer",
    )(tokens, experts.T, mix_weight.T, w_gate, w_up, w_down)


def solution(mesh):
    placed = (
        P("group", None),
        P("group", None),
        P("group", None),
        P("group", None, "shard"),
        P("group", None, "shard"),
        P("group", "shard", None),
    )
    return jax.shard_map(
        local, mesh=mesh, in_specs=placed, out_specs=P("group", "shard"), check_vma=False
    )
```

time: 250 us -> 90.8 us (0.36)
  waiting for transfers between devices: 90.7 us -> 0 us
  Pallas kernels: 0 us -> 89.1 us
  blocking collectives: 77.8 us -> 0 us
  local copies, waits for them, and re-layouts: 44.2 us -> 1.54 us
  between operations: 13.6 us -> 0.01 us
  matrix products: 12.2 us -> 0 us
  other arithmetic: 5.8 us -> 0 us
  starting transfers between devices: 4.27 us -> 0 us
    pallas_call x0 -> x1, Pallas kernels: none -> 89.1 us  [local(): pl.pallas_call(kernel, out_shape=jax.ShapeDtypeStruct((TG, 384), BF16), i...]
    unnamed x2 -> x0, waiting for transfers between devices: 82 us -> none
    all_to_all x1 -> x0, blocking collectives: 77.8 us -> none  [local(): lax.all_to_all(outgoing, 'group', split_axis=0, concat_axis=0, tiled=True)]
    unnamed x24 -> x1, local copies, waits for them, and re-layouts: 35.3 us -> 1.54 us
    dot_general x3 -> x0, matrix products: 12.2 us -> none  [the longest x1 5.36 us: local(): jnp.dot(hidden, w_down[0], preferred_element_type=jnp.float32)]
    all_to_all x1 -> x0, waiting for transfers between devices: 8.67 us -> none  [local(): lax.all_to_all(summed, 'group', split_axis=0, concat_axis=0, tiled=True)]
    gather x2 -> x0, local copies, waits for them, and re-layouts: 7.98 us -> none  [the longest x1 6.09 us: local(): tokens[source_row]]
    all_to_all x1 -> x0, starting transfers between devices: 4.27 us -> none  [local(): lax.all_to_all(summed, 'group', split_axis=0, concat_axis=0, tiled=True)]
  transfers between devices with their start and end apart: 2 -> 0, of which waited for: 2 -> 0; matrix products, arithmetic and copies ran while one was open for 0% -> 0% of each run, Pallas kernels for 0% -> 0%
where the time goes in v1:
time: 90.8 us; the launch traced here: 90.6 us
  Pallas kernels  89.1 us (98%)
  local copies, waits for them, and re-layouts  1.54 us (2%)
    pallas_call x1, Pallas kernels, local(): pl.pallas_call(kernel, out_shape=jax.ShapeDtypeStruct((TG, 384), BF16), i...  89.1 us

profile of v1, /device:TPU:0, one launch (start us, length us, event | category | flops | bytes accessed | tf_op | source)
XLA Modules:
  0.0 90.6 jit_solution(14130272842216681073)
XLA Ops:
  0.0 89.1 %expert_layer.1 = bf16[128,384]{1,0:T(8,128)(2,1)} custom-call(bf16[128,6144]{1,0:T(8,128)(2,1)} %tok.1, s32[2,128]{1,0:T(2,128)} %bitcast.2, f32[2,128]{1,0:T(2,128)} %bitcast.3, bf16[1,6144,512]{2,1,0:T(8,128)(2,1)} %wg_hbm.1, bf16[1,6144,512]{2,1,0:T(8,128)(2,1)} %wu_hbm.1, bf16[1,512,6144]{2,1,0:T(8,128)(2,1)} %wd_hbm.1), custom_call_target="tpu_custom_call" | custom-call | tf_op jit(solution)/shard_map/expert_layer/pallas_call | solution.py:370
  89.1 1.5 %copy.8 = bf16[128,384]{1,0:T(8,128)(2,1)} copy(bf16[128,384]{1,0:T(8,128)(2,1)} %expert_layer.1) | data formatting | bytes 196608

commit v2 on v1

--- a/solution.py
+++ b/solution.py
@@ -15,7 +15,8 @@
 KB = 768
 FFS = 512
 HALF = 3072
-CHUNKS = 2
+CHUNKS = 4
+LAG = 2
 ROWS = TG // CHUNKS
 COLS = 512
 
@@ -88,18 +89,22 @@
         return tok.at[pl.ds(h * ROWS, ROWS), pl.ds(pl.multiple_of(core * HALF + q * KB, KB), KB)]
 
     direct = {}
-    for h in range(CHUNKS):
+
+    def send_along_y(h, d, copies):
         for step in (1, -1):
             for dc in range(2):
                 core = c if dc == 0 else sib
-                q = ring_place(core)
-                direct[h, step, dc] = go(
+                q = (ring_place(core) + d) % NX
+                copies[h, step, dc] = go(
                     remote(
                         token_block(core, q, h),
                         land.at[q, y, c, pl.ds(h * ROWS, ROWS)],
                         dev(x, y + step + NX, z, core),
                     )
                 )
+
+    for h in range(CHUNKS):
+        send_along_y(h, 0, direct)
     load_g.start()
     load_u.start()
     across = [
@@ -113,7 +118,7 @@
 
     def load_down(i, carry):
         j, b = i // 16, i % 16
-        place = jnp.where(j == 2, (b % NX) * NX + b // NX, b)
+        place = jnp.where(j == 0, b, (b % NX) * NX + b // NX)
         pltpu.make_async_copy(
             wd_hbm.at[0, :, pl.ds(pl.multiple_of(b * 384 + j * 128, 128), 128)],
             wd.at[j, :, pl.ds(pl.multiple_of(place * 128, 128), 128)],
@@ -122,6 +127,8 @@
         return carry
 
     lax.fori_loop(0, 48, load_down, 0)
+
+    STEPS = ((0, 2), (1, 3))
 
     for copy in plans:
         copy.wait_recv()
@@ -138,21 +145,29 @@
         rank = jnp.dot(named.astype(BF16), before, preferred_element_type=F32)
         plan.append(jnp.where(named > 0.5, rank, -1.0))
     weight = jnp.where(first == own_e, first_w, 0.0) + jnp.where(second == own_e, second_w, 0.0)
-    for g in range(8):
-        py, pc = g // 2, g % 2
-        rows = [jnp.where(p[g : g + 1, :] == slot, 1.0, 0.0) for p in plan]
-        onehot = jnp.concatenate(rows, axis=0)
-        pick[g] = onehot.astype(BF16)
-        back[pc, py] = onehot.T.astype(BF16)
-        total = jnp.sum(rows[0] * weight[g : g + 1, :], axis=1, keepdims=True)
-        wslot[pl.ds((pc * 4 + py) * CAP, CAP)] = jnp.broadcast_to(total, (CAP, 128))
-
-    ring_own, relay_y, ring_relay = {}, {}, {}
+    for py in range(NX):
+        for pc in range(2):
+            g = 2 * py + pc
+            rows = [jnp.where(p[g : g + 1, :] == slot, 1.0, 0.0) for p in plan]
+            onehot = jnp.concatenate(rows, axis=0)
+            pick[g] = onehot.astype(BF16)
+            back[pc, py] = onehot.T.astype(BF16)
+            total = jnp.sum(rows[0] * weight[g : g + 1, :], axis=1, keepdims=True)
+            wslot[g] = jnp.broadcast_to(total, (CAP, 128))
+
+    ring_own, relay_y, ring_relay, wide = {}, {}, {}, {}
 
     def forward(h, dy):
         block = land.at[r, (y + dy) % NX, :, pl.ds(h * ROWS, ROWS)]
         for d in (1, -1):
             ring_own[h, dy, d] = go(remote(block, block, on_ring(d)))
+
+    def pass_on(h, dy):
+        for d in (1, -1):
+            ring_own[h, dy, d].wait_recv()
+            if dy == 2:
+                block = land.at[(r - d + NX) % NX, (y + dy) % NX, 1 if d == 1 else 0, pl.ds(h * ROWS, ROWS)]
+                ring_relay[h, dy, d] = go(remote(block, block, on_ring(d)))
 
     for h in range(CHUNKS):
         for dy, step in ((3, 1), (1, -1)):
@@ -161,19 +176,8 @@
             block = land.at[r, (y + dy) % NX, 1 if step == 1 else 0, pl.ds(h * ROWS, ROWS)]
             relay_y[h, step] = go(remote(block, block, dev(x, y + step + NX, z, c)))
             forward(h, dy)
-
-    def pass_on(h, dy):
-        for d in (1, -1):
-            ring_own[h, dy, d].wait_recv()
-            block = land.at[(r - d + NX) % NX, (y + dy) % NX, 1 if d == 1 else 0, pl.ds(h * ROWS, ROWS)]
-            ring_relay[h, dy, d] = go(remote(block, block, on_ring(d)))
-
-    for h in range(CHUNKS):
-        for step in (1, -1):
-            relay_y[h, step].wait_recv()
-        forward(h, 2)
-        for dy in (3, 1):
-            pass_on(h, dy)
+    for h in range(CHUNKS):
+        send_along_y(h, 2, wide)
     for copy in own_loads:
         copy.wait()
     for copy in across:
@@ -181,68 +185,82 @@
     load_g.wait()
     load_u.wait()
 
-    acc_g[...] = jnp.zeros_like(acc_g)
-    acc_u[...] = jnp.zeros_like(acc_u)
-    cross = []
-
-    def select(i, q):
-        def one(g, carry):
-            py, pc = g // 2, g % 2
-            rows = jnp.dot(pick[g], land[q, py, pc], preferred_element_type=F32).astype(BF16)
-            place = pl.ds(pl.multiple_of((pc * 4 + py) * CAP, CAP), CAP)
+    cross = {}
+
+    def select(i, q, half):
+        for g in range(4):
+            k, pc = g % 2, g // 2
+            py = (y + 2 * k + half) % NX
+            rows = jnp.dot(pick[2 * py + pc], land[q, py, pc], preferred_element_type=F32).astype(BF16)
+            place = pl.ds(half * 256 + g * CAP, CAP)
             xown[place, :] = rows[0:CAP]
             xsend[i, place, :] = rows[CAP:]
-            return carry
-
-        lax.fori_loop(0, 8, one, 0)
-        cross.append(go(remote(xsend.at[i], xsib.at[i], dev(x, y, z, sib))))
-
-    def gate_up(rows_ref, start):
+
+        part = pl.ds(half * 256, 256)
+        cross[i, half] = go(remote(xsend.at[i, part], xsib.at[i, part], dev(x, y, z, sib)))
+
+    def gate_up(rows_ref, start, half, fresh):
         depth = pl.ds(pl.multiple_of(start, KB), KB)
-
-        def one(m, carry):
-            place = pl.ds(pl.multiple_of(m * 256, 256), 256)
-            rows = rows_ref[place, :]
-            acc_g[place, :] += jnp.dot(rows, wg[depth, :], preferred_element_type=F32)
-            acc_u[place, :] += jnp.dot(rows, wu[depth, :], preferred_element_type=F32)
-            return carry
-
-        lax.fori_loop(0, 2, one, 0)
+        place = pl.ds(half * 256, 256)
+        rows = rows_ref[place, :]
+        for acc, w in ((acc_g, wg), (acc_u, wu)):
+            part = jnp.dot(rows, w[depth, :], preferred_element_type=F32)
+            if fresh:
+                acc[place, :] = part
+            else:
+                acc[place, :] += part
 
     order = (0, 1, 3, 2)
     places = [(r + d) % NX for d in order]
     sib_places = [(ring_place(sib) + d) % NX for d in order]
 
-    def own_block(i):
-        select(i, places[i])
-        gate_up(xown, c * HALF + places[i] * KB)
-
-    def sib_block(i):
-        cross[i].wait_recv()
-        gate_up(xsib.at[i], sib * HALF + sib_places[i] * KB)
-
-    own_block(0)
+    def own_block(i, half):
+        select(i, places[i], half)
+        gate_up(xown, c * HALF + places[i] * KB, half, i == 0)
+
+    def sib_block(i, half):
+        cross[i, half].wait_recv()
+        gate_up(xsib.at[i], sib * HALF + sib_places[i] * KB, half, False)
+
+    def activate(half):
+        for g in range(4):
+            k, pc = g % 2, g // 2
+            place = pl.ds(half * 256 + g * CAP, CAP)
+            gate, up = acc_g[place, :], acc_u[place, :]
+            scale = wslot[2 * ((y + 2 * k + half) % NX) + pc][:, 0:1]
+            hid[place, :] = (jax.nn.silu(gate) * up * scale).astype(BF16)
+
+    own_block(0, 1)
+    for h in range(CHUNKS):
+        for step in (1, -1):
+            relay_y[h, step].wait_recv()
+        forward(h, 2)
+    own_block(0, 0)
+    for h in range(CHUNKS):
+        for dy in (3, 1):
+            pass_on(h, dy)
+    sib_block(0, 1)
+    own_block(1, 1)
     for h in range(CHUNKS):
         pass_on(h, 2)
-    own_block(1)
-    own_block(2)
-    sib_block(0)
-    sib_block(1)
-    for h in range(CHUNKS):
-        for dy in (3, 1, 2):
-            for d in (1, -1):
-                ring_relay[h, dy, d].wait_recv()
-    own_block(3)
-    sib_block(2)
-    sib_block(3)
-
-    def activate(m, carry):
-        place = pl.ds(pl.multiple_of(m * 128, 128), 128)
-        gate, up = acc_g[place, :], acc_u[place, :]
-        hid[place, :] = (jax.nn.silu(gate) * up * wslot[place, 0:1]).astype(BF16)
-        return carry
-
-    lax.fori_loop(0, 4, activate, 0)
+    own_block(2, 1)
+    own_block(1, 0)
+    own_block(2, 0)
+    sib_block(0, 0)
+    sib_block(1, 1)
+    sib_block(2, 1)
+    for copy in ring_relay.values():
+        copy.wait_recv()
+    own_block(3, 0)
+    sib_block(1, 0)
+    sib_block(2, 0)
+    for copy in wide.values():
+        copy.wait_recv()
+    own_block(3, 1)
+    sib_block(3, 0)
+    activate(0)
+    sib_block(3, 1)
+    activate(1)
 
     pltpu.make_async_copy(wd, wd, local_sem.at[2]).wait()
     ts = (t0, t1, t2)
@@ -257,22 +275,26 @@
     def down(n, j, a):
         columns = pl.ds(pl.multiple_of(a * COLS, COLS), COLS)
         w = wd[j, :, columns]
-        theirs = jnp.dot(hid[pl.ds(pl.multiple_of(sib * 256, 256), 256), :], w, preferred_element_type=F32)
-        psend[n] = theirs.astype(BF16).reshape(4, CAP, COLS)
+        def rows_of(core):
+            first, second = (pl.ds(pl.multiple_of(half * 256 + core * 128, 128), 128) for half in range(2))
+            rows = jnp.concatenate([hid[first, :], hid[second, :]], axis=0)
+            return jnp.dot(rows, w, preferred_element_type=F32).astype(BF16).reshape(4, CAP, COLS)
+
+        psend[n] = rows_of(sib)
         swap[n] = go(remote(psend.at[n], pcat.at[n, :, pl.ds(CAP, CAP), :], dev(x, y, z, sib)))
-        ours = jnp.dot(hid[pl.ds(pl.multiple_of(c * 256, 256), 256), :], w, preferred_element_type=F32)
-        pcat[n, :, 0:CAP, :] = ours.astype(BF16).reshape(4, CAP, COLS)
+        pcat[n, :, 0:CAP, :] = rows_of(c)
 
     def combine(n, j, a):
         swap[n].wait_recv()
-        for py in range(4):
-            rows = jnp.dot(back[c, py], pcat[n, py], preferred_element_type=F32).astype(BF16)
+        for i in range(4):
+            py = (y + STEPS[i // 2][i % 2]) % NX
+            rows = jnp.dot(back[c, py], pcat[n, i], preferred_element_type=F32).astype(BF16)
             for b in range(4):
                 part = rows[:, b * 128 : (b + 1) * 128]
                 if j == 0:
                     t0[a, py, b] = part
                 elif j == 1:
-                    t1[py, b, a] = part
+                    t1[py, a, b] = part
                 else:
                     t2[a, b, py] = part
 
@@ -305,13 +327,6 @@
         add(t, (place + 3) % NX, size, size, buf.at[j, 1])
         start(j, level, t, buf, place, axis, "L2")
 
-    def finish(j, level, t, buf, place, axis):
-        size = t.shape[1] // 2
-        for kind in ("R1b", "L1b", "R2", "L2"):
-            copies[j, level, kind].wait_recv()
-        add(t, place, 0, size, buf.at[j, 4], buf.at[j, 3])
-        add(t, place, size, size, buf.at[j, 2], buf.at[j, 5])
-
     axes = ((0, 1, 2), (1, 2, 0), (2, 0, 1))
 
     def args(j, level):
@@ -320,14 +335,13 @@
             t = t.at[at[j][l]]
         return (j, level, t, (rb1, rb2, rb3)[level], at[j][level], axes[j][level])
 
-    chunks = [(1, 0, 0), (1, 0, 1), (1, 0, 2), (1, 0, 3)]
-    chunks += [(0, x, 2), (2, z, 2), (0, x, 1), (0, x, 3), (2, z, 1), (2, z, 3), (0, x, 0), (2, z, 0)]
+    chunks = [(1, 0, 0), (1, 0, 1), (0, x, 2), (2, z, 2), (1, 0, 2), (1, 0, 3)]
+    chunks += [(0, x, 1), (0, x, 3), (2, z, 1), (2, z, 3), (0, x, 0), (2, z, 0)]
 
     def after(j, k):
         if j == 1:
-            if k == 3:
-                for kind in ("R1a", "L1a", "R1b", "L1b"):
-                    start(*args(1, 0), kind)
+            for kind in {1: ("R1a", "L1b"), 3: ("L1a", "R1b")}.get(k, ()):
+                start(*args(1, 0), kind)
         elif k == 2:
             start(*args(j, 0), "R1a")
             start(*args(j, 0), "L1a")
@@ -336,32 +350,56 @@
         elif k == 3:
             start(*args(j, 0), "L1b")
 
-    lag = 1
-    for n in range(len(chunks) + lag):
+    for n in range(len(chunks) + LAG):
         if n < len(chunks):
             j, base, k = chunks[n]
             down(n, j, (base + k) % NX)
-        if n >= lag:
-            j, base, k = chunks[n - lag]
-            combine(n - lag, j, (base + k) % NX)
+        if n >= LAG:
+            j, base, k = chunks[n - LAG]
+            combine(n - LAG, j, (base + k) % NX)
             after(j, k)
 
-    for level in range(3):
-        if level:
-            for j in (1, 0, 2):
-                for kind in ("R1a", "L1a", "R1b", "L1b"):
-                    start(*args(j, level), kind)
-        for j in (1, 0, 2):
-            middle(*args(j, level))
-        for j in (1, 0, 2):
-            finish(*args(j, level))
-    for j in range(3):
-        out[:, j * 128 : (j + 1) * 128] = ts[j][at[j][0], at[j][1], at[j][2]]
+    straight = {}
+
+    def spread(j, level, d):
+        _, _, t, buf, place, axis = args(j, level)
+        straight[j, level, d] = go(remote(t.at[(place + d) % NX], buf.at[j, d - 1], steps[axis](d)))
+
+    def gather(j, level):
+        _, _, t, buf, place, _ = args(j, level)
+        total = t[place].astype(F32)
+        for d in (1, 2, 3):
+            straight[j, level, d].wait_recv()
+            total = total + buf[j, d - 1].astype(F32)
+        return total
+
+    def finish(j):
+        for kind in ("R1b", "L1b", "R2", "L2"):
+            copies[j, 0, kind].wait_recv()
+        here, second = ts[j].at[at[j][0]], at[j][1]
+        for d in (2, 1, 3, 0):
+            b = (second + d) % NX
+            one, two = jnp.where(b < 2, 4, 2), jnp.where(b < 2, 3, 5)
+            total = here[b].astype(F32) + rb1[j, one, b % 2].astype(F32) + rb1[j, two, b % 2].astype(F32)
+            here[b] = total.astype(BF16)
+            if d:
+                spread(j, 1, d)
+
+    for j in (1, 0, 2):
+        middle(*args(j, 0))
+    for j in (1, 0, 2):
+        finish(j)
+    for j in (1, 0, 2):
+        ts[j][at[j][0], at[j][1]] = gather(j, 1).astype(BF16)
+        for d in (2, 1, 3):
+            spread(j, 2, d)
+    for j in (1, 0, 2):
+        out[:, j * 128 : (j + 1) * 128] = gather(j, 2).astype(BF16)
     for copy in sent:
         copy.wait_send()
 
 
-MESSAGES = 7 + 4 * CHUNKS + 4 + 2 * CHUNKS + 6 * CHUNKS + 6 * CHUNKS + 4 + 12 + 54
+MESSAGES = 7 + 4 * CHUNKS + 4 + 2 * CHUNKS + 6 * CHUNKS + 6 * CHUNKS + 8 + 12 + 36
 
 
 def local(tokens, experts, mix_weight, w_gate, w_up, w_down):
@@ -380,7 +418,7 @@
             pltpu.VMEM((8, 8, TG), F32),
             pltpu.VMEM((8, TG, TG), BF16),
             pltpu.VMEM((2, 4, TG, TG), BF16),
-            pltpu.VMEM((512, 128), F32),
+            pltpu.VMEM((8, CAP, 128), F32),
             pltpu.VMEM((512, KB), BF16),
             pltpu.VMEM((4, 512, KB), BF16),
             pltpu.VMEM((4, 512, KB), BF16),
@@ -393,8 +431,8 @@
             pltpu.VMEM((4, 4, 4, 128, 128), BF16),
             pltpu.VMEM((4, 4, 4, 128, 128), BF16),
             pltpu.VMEM((3, 6, 2, 4, 128, 128), BF16),
-            pltpu.VMEM((3, 6, 2, 128, 128), BF16),
-            pltpu.VMEM((3, 6, 64, 128), BF16),
+            pltpu.VMEM((3, 3, 4, 128, 128), BF16),
+            pltpu.VMEM((3, 3, 128, 128), BF16),
             pltpu.SemaphoreType.DMA((7,)),
             pltpu.SemaphoreType.DMA((MESSAGES,)),
             pltpu.SemaphoreType.DMA((MESSAGES,)),

time: 90.8 us -> 77.1 us (0.85)
  Pallas kernels: 89.1 us -> 75.4 us
    pallas_call x1, Pallas kernels: 89.1 us -> 75.4 us  [local(): pl.pallas_call(kernel, out_shape=jax.ShapeDtypeStruct((TG, 384), BF16), i...]
where the time goes in v2:
time: 77.1 us; the launch traced here: 77 us
  Pallas kernels  75.4 us (98%)
  local copies, waits for them, and re-layouts  1.54 us (2%)
    pallas_call x1, Pallas kernels, local(): pl.pallas_call(kernel, out_shape=jax.ShapeDtypeStruct((TG, 384), BF16), i...  75.4 us
    unnamed x1, local copies, waits for them, and re-layouts  1.54 us

profile of v2, /device:TPU:0, one launch (start us, length us, event | category | flops | bytes accessed | tf_op | source)
XLA Modules:
  0.0 77.0 jit_solution(9689761013832788379)
XLA Ops:
  0.0 75.4 %expert_layer.1 = bf16[128,384]{1,0:T(8,128)(2,1)} custom-call(bf16[128,6144]{1,0:T(8,128)(2,1)} %tok.1, s32[2,128]{1,0:T(2,128)} %bitcast.2, f32[2,128]{1,0:T(2,128)} %bitcast.3, bf16[1,6144,512]{2,1,0:T(8,128)(2,1)} %wg_hbm.1, bf16[1,6144,512]{2,1,0:T(8,128)(2,1)} %wu_hbm.1, bf16[1,512,6144]{2,1,0:T(8,128)(2,1)} %wd_hbm.1), custom_call_target="tpu_custom_call" | custom-call | tf_op jit(solution)/shard_map/expert_layer/pallas_call | solution.py:408
  75.4 1.5 %copy.8 = bf16[128,384]{1,0:T(8,128)(2,1)} copy(bf16[128,384]{1,0:T(8,128)(2,1)} %expert_layer.1) | data formatting | bytes 196608

commit v3 on v2

--- a/solution.py
+++ b/solution.py
@@ -239,14 +239,16 @@
     for h in range(CHUNKS):
         for dy in (3, 1):
             pass_on(h, dy)
+    pass_on(0, 2)
+    own_block(1, 1)
+    pass_on(1, 2)
+    own_block(2, 1)
+    pass_on(2, 2)
     sib_block(0, 1)
-    own_block(1, 1)
-    for h in range(CHUNKS):
-        pass_on(h, 2)
-    own_block(2, 1)
+    pass_on(3, 2)
+    sib_block(0, 0)
     own_block(1, 0)
     own_block(2, 0)
-    sib_block(0, 0)
     sib_block(1, 1)
     sib_block(2, 1)
     for copy in ring_relay.values():
@@ -299,33 +301,32 @@
                     t2[a, b, py] = part
 
     copies = {}
-
-    def start(j, level, t, buf, place, axis, kind):
-        size = t.shape[1] // 2
-        far, right, left = (place + 2) % NX, (place + 1) % NX, (place + 3) % NX
-        low, high = pl.ds(0, size), pl.ds(size, size)
-        src = {
-            "R1a": t.at[far, low], "L1a": t.at[far, high], "R1b": t.at[right, high],
-            "L1b": t.at[left, low], "R2": t.at[right, low], "L2": t.at[left, high],
+    kinds = ("R1a", "L1a", "R1b", "L1b", "R2", "L2")
+    low, high = pl.ds(0, 2), pl.ds(2, 2)
+    SPLIT = (pl.ds(0, 64), pl.ds(64, 64))
+
+    def start(j, kind, rows=pl.ds(0, 128), s=0):
+        t, place, axis = ts[j], at[j][0], axes[j][0]
+        d, half = {
+            "R1a": (2, low), "L1a": (2, high), "R1b": (1, high), "L1b": (3, low), "R2": (1, low), "L2": (3, high),
         }[kind]
-        slot_of = ("R1a", "L1a", "R1b", "L1b", "R2", "L2").index(kind)
-        copies[j, level, kind] = go(remote(src, buf.at[j, slot_of], steps[axis](1 if kind[0] == "R" else -1)))
-
-    def add(t, index, low, size, *bufs):
-        place = pl.ds(low, size)
-        total = t[index, place].astype(F32)
-        for buf in bufs:
-            total = total + buf[...].astype(F32)
-        t[index, place] = total.astype(BF16)
-
-    def middle(j, level, t, buf, place, axis):
-        size = t.shape[1] // 2
-        copies[j, level, "R1a"].wait_recv()
-        add(t, (place + 1) % NX, 0, size, buf.at[j, 0])
-        start(j, level, t, buf, place, axis, "R2")
-        copies[j, level, "L1a"].wait_recv()
-        add(t, (place + 3) % NX, size, size, buf.at[j, 1])
-        start(j, level, t, buf, place, axis, "L2")
+        copies[j, kind, s] = go(
+            remote(
+                t.at[(place + d) % NX, half, :, rows],
+                rb1.at[j, kinds.index(kind), :, :, rows],
+                steps[axis](1 if kind[0] == "R" else -1),
+            )
+        )
+
+    def middle(j, kind):
+        t, place = ts[j], at[j][0]
+        copies[j, kind, 0].wait_recv()
+        d, half, slot_of, on = (1, low, 0, "R2") if kind == "R1a" else (3, high, 1, "L2")
+        for s, rows in enumerate(SPLIT):
+            index = (place + d) % NX
+            total = t[index, half, :, rows].astype(F32) + rb1[j, slot_of, :, :, rows].astype(F32)
+            t[index, half, :, rows] = total.astype(BF16)
+            start(j, on, rows, s)
 
     axes = ((0, 1, 2), (1, 2, 0), (2, 0, 1))
 
@@ -341,14 +342,14 @@
     def after(j, k):
         if j == 1:
             for kind in {1: ("R1a", "L1b"), 3: ("L1a", "R1b")}.get(k, ()):
-                start(*args(1, 0), kind)
+                start(1, kind)
         elif k == 2:
-            start(*args(j, 0), "R1a")
-            start(*args(j, 0), "L1a")
+            start(j, "R1a")
+            start(j, "L1a")
         elif k == 1:
-            start(*args(j, 0), "R1b")
+            start(j, "R1b")
         elif k == 3:
-            start(*args(j, 0), "L1b")
+            start(j, "L1b")
 
     for n in range(len(chunks) + LAG):
         if n < len(chunks):
@@ -361,45 +362,57 @@
 
     straight = {}
 
-    def spread(j, level, d):
+    def spread(j, level, d, s):
         _, _, t, buf, place, axis = args(j, level)
-        straight[j, level, d] = go(remote(t.at[(place + d) % NX], buf.at[j, d - 1], steps[axis](d)))
-
-    def gather(j, level):
+        lead = (slice(None),) * (level == 1)
+        index = (place + d) % NX
+        straight[j, level, d, s] = go(
+            remote(t.at[(index, *lead, SPLIT[s])], buf.at[(j, d - 1, *lead, SPLIT[s])], steps[axis](d))
+        )
+
+    def gather(j, level, s):
         _, _, t, buf, place, _ = args(j, level)
-        total = t[place].astype(F32)
+        lead = (slice(None),) * (level == 1)
+        total = t[(place, *lead, SPLIT[s])].astype(F32)
         for d in (1, 2, 3):
-            straight[j, level, d].wait_recv()
-            total = total + buf[j, d - 1].astype(F32)
-        return total
-
-    def finish(j):
-        for kind in ("R1b", "L1b", "R2", "L2"):
-            copies[j, 0, kind].wait_recv()
-        here, second = ts[j].at[at[j][0]], at[j][1]
+            straight[j, level, d, s].wait_recv()
+            total = total + buf[(j, d - 1, *lead, SPLIT[s])].astype(F32)
+        return total.astype(BF16)
+
+    def finish(j, s):
+        if s == 0:
+            copies[j, "R1b", 0].wait_recv()
+            copies[j, "L1b", 0].wait_recv()
+        copies[j, "R2", s].wait_recv()
+        copies[j, "L2", s].wait_recv()
+        here, second, rows = ts[j].at[at[j][0]], at[j][1], SPLIT[s]
         for d in (2, 1, 3, 0):
             b = (second + d) % NX
             one, two = jnp.where(b < 2, 4, 2), jnp.where(b < 2, 3, 5)
-            total = here[b].astype(F32) + rb1[j, one, b % 2].astype(F32) + rb1[j, two, b % 2].astype(F32)
-            here[b] = total.astype(BF16)
+            total = here[b, :, rows].astype(F32)
+            total = total + rb1[j, one, b % 2, :, rows].astype(F32) + rb1[j, two, b % 2, :, rows].astype(F32)
+            here[b, :, rows] = total.astype(BF16)
             if d:
-                spread(j, 1, d)
-
-    for j in (1, 0, 2):
-        middle(*args(j, 0))
-    for j in (1, 0, 2):
-        finish(j)
-    for j in (1, 0, 2):
-        ts[j][at[j][0], at[j][1]] = gather(j, 1).astype(BF16)
-        for d in (2, 1, 3):
-            spread(j, 2, d)
-    for j in (1, 0, 2):
-        out[:, j * 128 : (j + 1) * 128] = gather(j, 2).astype(BF16)
+                spread(j, 1, d, s)
+
+    for j, kind in ((1, "R1a"), (0, "R1a"), (0, "L1a"), (2, "R1a"), (2, "L1a"), (1, "L1a")):
+        middle(j, kind)
+    for s in range(2):
+        for j in (0, 2, 1):
+            finish(j, s)
+    for s in range(2):
+        for j in (0, 2, 1):
+            ts[j][at[j][0], at[j][1], :, SPLIT[s]] = gather(j, 1, s)
+            for d in (2, 1, 3):
+                spread(j, 2, d, s)
+    for s in range(2):
+        for j in (0, 2, 1):
+            out[SPLIT[s], j * 128 : (j + 1) * 128] = gather(j, 2, s)
     for copy in sent:
         copy.wait_send()
 
 
-MESSAGES = 7 + 4 * CHUNKS + 4 + 2 * CHUNKS + 6 * CHUNKS + 6 * CHUNKS + 8 + 12 + 36
+MESSAGES = 7 + 4 * CHUNKS + 4 + 2 * CHUNKS + 6 * CHUNKS + 6 * CHUNKS + 8 + 12 + 60
 
 
 def local(tokens, experts, mix_weight, w_gate, w_up, w_down):

time: 77.1 us -> 74.8 us (0.970)
  Pallas kernels: 75.4 us -> 73.1 us
    pallas_call x1, Pallas kernels: 75.4 us -> 73.1 us  [local(): pl.pallas_call(kernel, out_shape=jax.ShapeDtypeStruct((TG, 384), BF16), i...]
where the time goes in v3:
time: 74.8 us; the launch traced here: 74.6 us
  Pallas kernels  73.1 us (98%)
  local copies, waits for them, and re-layouts  1.54 us (2%)
    pallas_call x1, Pallas kernels, local(): pl.pallas_call(kernel, out_shape=jax.ShapeDtypeStruct((TG, 384), BF16), i...  73.1 us
    unnamed x1, local copies, waits for them, and re-layouts  1.54 us

profile of v3, /device:TPU:0, one launch (start us, length us, event | category | flops | bytes accessed | tf_op | source)
XLA Modules:
  0.0 74.6 jit_solution(3936366118870925765)
XLA Ops:
  0.0 73.1 %expert_layer.1 = bf16[128,384]{1,0:T(8,128)(2,1)} custom-call(bf16[128,6144]{1,0:T(8,128)(2,1)} %tok.1, s32[2,128]{1,0:T(2,128)} %bitcast.2, f32[2,128]{1,0:T(2,128)} %bitcast.3, bf16[1,6144,512]{2,1,0:T(8,128)(2,1)} %wg_hbm.1, bf16[1,6144,512]{2,1,0:T(8,128)(2,1)} %wu_hbm.1, bf16[1,512,6144]{2,1,0:T(8,128)(2,1)} %wd_hbm.1), custom_call_target="tpu_custom_call" | custom-call | tf_op jit(solution)/shard_map/expert_layer/pallas_call | solution.py:421
  73.1 1.5 %copy.8 = bf16[128,384]{1,0:T(8,128)(2,1)} copy(bf16[128,384]{1,0:T(8,128)(2,1)} %expert_layer.1) | data formatting | bytes 196608

commit v4 on v3

--- a/solution.py
+++ b/solution.py
@@ -58,6 +58,11 @@
         copy.start()
         sent.append(copy)
         return copy
+
+    def drain(upto=None):
+        for copy in sent[:upto]:
+            copy.wait_send()
+        del sent[:upto]
 
     peers = [((y + dy) % NX, c if dc == 0 else sib) for dy in range(NX) for dc in range(2) if dy or dc]
     partners = [dev(x, py, z, pc) for py, pc in peers]
@@ -228,7 +233,7 @@
             place = pl.ds(half * 256 + g * CAP, CAP)
             gate, up = acc_g[place, :], acc_u[place, :]
             scale = wslot[2 * ((y + 2 * k + half) % NX) + pc][:, 0:1]
-            hid[place, :] = (jax.nn.silu(gate) * up * scale).astype(BF16)
+            hid[pl.ds(pc * 256 + half * 128 + k * CAP, CAP), :] = (jax.nn.silu(gate) * up * scale).astype(BF16)
 
     own_block(0, 1)
     for h in range(CHUNKS):
@@ -264,6 +269,8 @@
     sib_block(3, 1)
     activate(1)
 
+    dispatched = len(sent)
+
     pltpu.make_async_copy(wd, wd, local_sem.at[2]).wait()
     ts = (t0, t1, t2)
     at = ((x, y, z), (y, z, x), (z, x, y))
@@ -278,8 +285,7 @@
         columns = pl.ds(pl.multiple_of(a * COLS, COLS), COLS)
         w = wd[j, :, columns]
         def rows_of(core):
-            first, second = (pl.ds(pl.multiple_of(half * 256 + core * 128, 128), 128) for half in range(2))
-            rows = jnp.concatenate([hid[first, :], hid[second, :]], axis=0)
+            rows = hid[pl.ds(pl.multiple_of(core * 256, 256), 256), :]
             return jnp.dot(rows, w, preferred_element_type=F32).astype(BF16).reshape(4, CAP, COLS)
 
         psend[n] = rows_of(sib)
@@ -395,21 +401,25 @@
             if d:
                 spread(j, 1, d, s)
 
+    drain(dispatched)
+    first_hops = len(sent)
     for j, kind in ((1, "R1a"), (0, "R1a"), (0, "L1a"), (2, "R1a"), (2, "L1a"), (1, "L1a")):
         middle(j, kind)
+    drain(first_hops)
+    second_hops = len(sent)
     for s in range(2):
         for j in (0, 2, 1):
             finish(j, s)
+    drain(second_hops)
     for s in range(2):
         for j in (0, 2, 1):
             ts[j][at[j][0], at[j][1], :, SPLIT[s]] = gather(j, 1, s)
             for d in (2, 1, 3):
                 spread(j, 2, d, s)
+    drain()
     for s in range(2):
         for j in (0, 2, 1):
             out[SPLIT[s], j * 128 : (j + 1) * 128] = gather(j, 2, s)
-    for copy in sent:
-        copy.wait_send()
 
 
 MESSAGES = 7 + 4 * CHUNKS + 4 + 2 * CHUNKS + 6 * CHUNKS + 6 * CHUNKS + 8 + 12 + 60

time: 74.8 us -> 74.5 us (level)
  no operation moved by 1% of the time
where the time goes in v4:
time: 74.5 us; the launch traced here: 74.4 us
  Pallas kernels  72.8 us (98%)
  local copies, waits for them, and re-layouts  1.54 us (2%)
    pallas_call x1, Pallas kernels, local(): pl.pallas_call(kernel, out_shape=jax.ShapeDtypeStruct((TG, 384), BF16), i...  72.8 us
    unnamed x1, local copies, waits for them, and re-layouts  1.54 us

profile of v4, /device:TPU:0, one launch (start us, length us, event | category | flops | bytes accessed | tf_op | source)
XLA Modules:
  0.0 74.4 jit_solution(10089651742249127618)
XLA Ops:
  0.0 72.8 %expert_layer.1 = bf16[128,384]{1,0:T(8,128)(2,1)} custom-call(bf16[128,6144]{1,0:T(8,128)(2,1)} %tok.1, s32[2,128]{1,0:T(2,128)} %bitcast.2, f32[2,128]{1,0:T(2,128)} %bitcast.3, bf16[1,6144,512]{2,1,0:T(8,128)(2,1)} %wg_hbm.1, bf16[1,6144,512]{2,1,0:T(8,128)(2,1)} %wu_hbm.1, bf16[1,512,6144]{2,1,0:T(8,128)(2,1)} %wd_hbm.1), custom_call_target="tpu_custom_call" | custom-call | tf_op jit(solution)/shard_map/expert_layer/pallas_call | solution.py:431
  72.8 1.5 %copy.8 = bf16[128,384]{1,0:T(8,128)(2,1)} copy(bf16[128,384]{1,0:T(8,128)(2,1)} %expert_layer.1) | data formatting | bytes 196608
